TPU v7x, 32 devices: a whole 2x2x4 slice. The times are simulated.
32 devices in a mesh: row: 8 (over y, x, core), col: 4 (over z).
Axes of the slice: x: 2, y: 2, z: 4, core: 2. Of those that a mesh axis runs over, the one named last changes fastest.
Arguments:
- telemetry: int32 [4096, 64], P(('col', 'row')), may hold values from -127 to 127
- scales: int32 [4096], P(('col', 'row')), may hold values from 1 to 4
- bands: int32 [2, 2], replicated, may hold values from 256 to 4096
- noise: float32 [4096], P('row'), may hold values from 0.5 to 2
- start: bfloat16 [4096, 64], P(('col', 'row')), may hold values from -6 to 6
- target: bfloat16 [4096, 64], P('row'), may hold values from -6 to 6
Outputs:
- first: float32 [4096, 64], P('row')
- second: float32 [4096, 64], P('row')
All inputs are finite; a program needn't handle non-finite values.
Results may differ from a plain program's by a relative error of at most 0.0023.
Values may be sent and summed in bfloat16 or wider, within the bound.
No kernel may reach another device: no remote copies, remote signals or barrier semaphores. Data moves between devices by JAX's collectives and lax.ppermute only.
A program may use at most 128 MiB of HBM per device.

v0:
```python
import math

import jax
import jax.numpy as jnp
from jax import lax
from jax.sharding import PartitionSpec as P

SUBAP = 2048


damping = 0.4


def from_root(block, axis, holder):
    block = jnp.where(lax.axis_index(axis) == holder, block, jnp.zeros_like(block))
    return lax.psum(block, axis)


def on_device(telemetry, scales, bands, noise, start, target):
    frame_count = telemetry.shape[1]
    row_count = lax.axis_size("row")
    col_count = lax.axis_size("col")
    ratio = row_count // col_count
    row_id = lax.axis_index("row")
    col_id = lax.axis_index("col")
    order_total = telemetry.shape[0] * row_count * col_count
    norm_count = jnp.float32(order_total // 4)
    slopes = (telemetry.astype(jnp.float32) * scales.astype(jnp.float32)[:, None] / 128.0).astype(
        jnp.bfloat16
    )
    joined = jnp.concatenate([slopes, start], axis=1)
    col_joined = lax.all_gather(joined, "row", axis=0, tiled=True)
    col_width = col_joined.shape[0]
    row_height = col_width // ratio
    half = lax.dynamic_slice_in_dim(col_joined, row_id % ratio * row_height, row_height, 0)
    row_joined = from_root(half, "col", row_id // ratio)
    row_slopes = row_joined[:, :frame_count]
    row_start = row_joined[:, frame_count:]
    col_slopes = col_joined[:, :frame_count]
    col_start = col_joined[:, frame_count:]
    panel_width = col_start.shape[1]
    row_f = row_slopes.astype(jnp.float32)
    weight = damping / (jnp.sum(row_f * row_f, axis=1) / norm_count + noise)
    count = bands.shape[0]
    index = jnp.arange(count, dtype=jnp.int32)
    sym = jnp.where(index[:, None] <= index[None, :], bands, bands.T).astype(jnp.float32)
    row_ids = row_id * row_height + jnp.arange(row_height, dtype=jnp.int32)
    onehot = (row_ids[:, None] // SUBAP == index[None, :]).astype(jnp.float32)
    row_band = jnp.dot(onehot, sym, precision=lax.Precision.HIGHEST)
    row_pos = (row_ids % SUBAP).astype(jnp.float32)
    width = math.gcd(math.gcd(col_width, 512), SUBAP)
    nblocks = col_width // width

    def build(step, carry):
        tile, acc = carry
        offset = step * width
        cols = lax.dynamic_slice_in_dim(col_slopes, offset, width, 0)
        raw = (
            lax.dot_general(
                row_slopes, cols, (((1,), (1,)), ((), ())), preferred_element_type=jnp.float32
            )
            / norm_count
        )
        col_ids = col_id * col_width + offset + jnp.arange(width, dtype=jnp.int32)
        band = lax.dynamic_slice_in_dim(row_band, (col_id * col_width + offset) // SUBAP, 1, 1)
        dist = jnp.abs(row_pos[:, None] - (col_ids % SUBAP).astype(jnp.float32)[None, :])
        taper = jnp.maximum(0.0, 1.0 - dist / band)
        diag = jnp.where(row_ids[:, None] == col_ids[None, :], noise[:, None], jnp.float32(0.0))
        entry = (taper * raw + diag).astype(jnp.bfloat16)
        tile = lax.dynamic_update_slice_in_dim(tile, entry, offset, 1)
        return (tile, acc)

    tile_init = jnp.zeros((row_height, col_width), jnp.bfloat16)
    acc_init = jnp.zeros((row_height, panel_width), jnp.float32)
    tile, acc = lax.fori_loop(0, nblocks, build, (tile_init, acc_init))
    product0 = jnp.dot(tile, col_start, preferred_element_type=jnp.float32)
    target_f = target.astype(jnp.float32)

    def refine(current, product):
        share = lax.psum_scatter(product, "col", scatter_dimension=0, tiled=True)
        share_rows = row_height // col_count
        begin = col_id * share_rows
        cur_part = lax.dynamic_slice_in_dim(current, begin, share_rows, 0)
        tgt_part = lax.dynamic_slice_in_dim(target_f, begin, share_rows, 0)
        wgt_part = lax.dynamic_slice_in_dim(weight, begin, share_rows, 0)
        updated = cur_part + wgt_part[:, None] * (tgt_part - share)
        return lax.all_gather(updated, "col", axis=0, tiled=True)

    first = refine(row_start.astype(jnp.float32), product0)
    first_low = first.astype(jnp.bfloat16)
    pieces = [from_root(first_low, "row", col_id * ratio + offset_q) for offset_q in range(ratio)]
    col_first = jnp.concatenate(pieces, axis=0)
    product1 = jnp.dot(tile, col_first, preferred_element_type=jnp.float32)
    second = refine(first, product1)
    return (first, second)


def solution(mesh):
    return jax.shard_map(
        on_device,
        mesh=mesh,
        in_specs=(
            P(("col", "row"), None),
            P(("col", "row")),
            P(),
            P("row"),
            P(("col", "row"), None),
            P("row", None),
        ),
        out_specs=(P("row", None), P("row", None)),
        check_vma=False,
    )
```

profile of v0, /device:TPU:0, one launch (start us, length us, event | category | flops | bytes accessed | tf_op | source)
XLA Modules:
  0.0 187.8 jit_solution(763219945140457815)
XLA Ops:
  7.2 0.0 copy-start.3
  7.2 0.0 all-reduce.4.cloned.1.call-start
  7.2 0.0 copy-start.8
  7.3 0.6 copy-done.8
  7.9 0.0 copy-done.3
  7.9 0.7 copy-done.5
  8.6 10.8 %all_gather.9 = bf16[1024,128]{0,1:T(8,128)(2,1)S(1)} all-gather(bf16[128,128]{0,1:T(8,128)(2,1)S(1)} %pad_maximum_fusion), channel_id=1, replica_groups=mesh['row'=8,'col'=4] {'row'}, dimensions={0}, use_global_device_ids=true | all-gather | bytes 294912 | tf_op jit(solution)/shard_map/all_gather | solution.py:32
  19.5 0.7 dynamic-slice_select_fusion
  20.2 0.0 all-reduce.4.cloned.1.call-update
  20.2 0.0 reduce-scatter.3.cloned.1.call-start
  20.3 0.0 copy-done
  20.3 0.0 copy-start.7
  20.3 0.7 copy-done.7
  21.0 0.1 copy.8
  21.1 0.3 fusion.15
  21.4 33.8 %all-reduce.4.cloned.1.call-done = bf16[512,128]{0,1:T(8,128)(2,1)} async-done(((bf16[512,128]{0,1:T(8,128)(2,1)}), bf16[512,128]{0,1:T(8,128)(2,1)}) %all-reduce.4.cloned.1.call-update) | async-done | bytes 131088 | tf_op jit(solution)/shard_map/psum | solution.py:16
  55.2 0.9 fusion.36
  56.0 0.1 copy.10
  56.2 0.0 slice-start
  56.2 0.0 copy-start.6
  56.2 0.1 broadcast_in_dim.50
  56.3 0.8 slice-done
  57.1 0.0 copy-done.6
  57.1 1.3 while.17
  57.1 0.5 fusion.49
  57.8 0.6 fusion.49
  58.3 0.0 copy-done.1
  58.4 1.0 fusion.16
  59.3 0.0 reduce-scatter.3.cloned.1.call-update
  59.3 0.0 copy-start.4
  59.3 0.0 all-reduce.6.cloned.1.call-start
  59.4 0.8 copy-done.2
  60.3 0.1 dynamic_slice.39
  60.3 18.0 %reduce-scatter.3.cloned.1.call-done = f32[128,64]{0,1:T(8,128)} async-done(((f32[512,64]{0,1:T(8,128)}), f32[128,64]{0,1:T(8,128)}) %reduce-scatter.3.cloned.1.call-update) | async-done | bytes 32784 | tf_op jit(solution)/shard_map/reduce_scatter | solution.py:80
  78.3 0.0 copy-done.4
  78.3 0.8 fusion.26
  79.1 13.4 %all_gather.10 = f32[512,64]{0,1:T(8,128)S(1)} all-gather(f32[128,64]{0,1:T(8,128)S(1)} %fusion.26), channel_id=1, replica_groups=mesh['row'=8,'col'=4] {'col'}, dimensions={0}, use_global_device_ids=true | all-gather | bytes 163840 | tf_op jit(solution)/shard_map/all_gather | solution.py:87
  92.4 0.7 broadcast_select_fusion.1
  93.1 0.0 all-reduce.6.cloned.1.call-update
  93.1 0.0 reduce-scatter.5.cloned.1.call-start
  93.2 51.4 %all-reduce.6.cloned.1.call-done = (bf16[512,64]{0,1:T(8,128)(2,1)}, bf16[512,64]{0,1:T(8,128)(2,1)}) async-done(((bf16[512,64]{0,1:T(8,128)(2,1)}, bf16[512,64]{0,1:T(8,128)(2,1)}), (bf16[512,64]{0,1:T(8,128)(2,1)}, bf16[512,64]{0,1:T(8,128)(2,1)})) %all-reduce.6.cloned.1.call-update) | async-done | bytes 131088 | tf_op jit(solution)/shard_map/psum | solution.py:16
  144.6 1.8 fusion.18
  146.4 0.0 reduce-scatter.5.cloned.1.call-update
  146.4 19.4 %reduce-scatter.5.cloned.1.call-done = f32[128,64]{0,1:T(8,128)} async-done(((f32[512,64]{0,1:T(8,128)}), f32[128,64]{0,1:T(8,128)}) %reduce-scatter.5.cloned.1.call-update) | async-done | bytes 32784 | tf_op jit(solution)/shard_map/reduce_scatter | solution.py:80
  165.8 0.8 fusion.24
  166.6 13.4 %all_gather.11 = f32[512,64]{0,1:T(8,128)S(1)} all-gather(f32[128,64]{0,1:T(8,128)S(1)} %fusion.24), channel_id=1, replica_groups=mesh['row'=8,'col'=4] {'col'}, dimensions={0}, use_global_device_ids=true | all-gather | bytes 163840 | tf_op jit(solution)/shard_map/all_gather | solution.py:87
  180.0 0.7 copy.24
  180.7 0.7 copy.25
  (16 shorter events, 0.1 us)
Async XLA Ops:
  7.2 0.8 copy-start.3
  7.2 48.0 %all-reduce.4.cloned.1.call-start = ((), (), s32[]{:S(2)}) async-start(), calls=%async_computation.2 | async-start | bytes 262144 | tf_op jit(solution)/shard_map/psum | solution.py:16
  7.2 0.7 copy-start.8
  7.9 0.7 copy-start.5
  19.5 0.8 copy-start
  20.2 58.1 %reduce-scatter.3.cloned.1.call-start = ((), (), s32[]{:S(2)}) async-start(), calls=%async_computation.3 | async-start | bytes 163840 | tf_op jit(solution)/shard_map/reduce_scatter | solution.py:80
  20.3 0.7 copy-start.7
  56.2 0.9 slice-start
  56.2 0.9 copy-start.6
  57.1 1.3 copy-start.1
  59.3 0.9 copy-start.2
  59.3 19.0 %copy-start.4 = (bf16[512,64]{0,1:T(8,128)(2,1)S(1)}, bf16[512,64]{0,1:T(8,128)(2,1)}, u32[]{:S(2)}) copy-start(bf16[512,64]{0,1:T(8,128)(2,1)} %param.13) | copy-start | bytes 196612
  59.3 85.2 %all-reduce.6.cloned.1.call-start = ((), (), s32[]{:S(2)}) async-start(), calls=%async_computation.5 | async-start | bytes 262144 | tf_op jit(solution)/shard_map/psum | solution.py:16
  93.1 72.7 %reduce-scatter.5.cloned.1.call-start = ((), (), s32[]{:S(2)}) async-start(), calls=%async_computation.4 | async-start | bytes 163840 | tf_op jit(solution)/shard_map/reduce_scatter | solution.py:80
Sparse Core Ops, SparseCore 0:
  20.3 34.7 all-reduce.3
  59.5 18.7 reduce-scatter.2
  93.2 51.2 all-reduce.5
  147.3 18.4 reduce-scatter.4
where the time goes:
time: 188 us
  waiting for transfers between devices  123 us (65%)
  blocking collectives  37.6 us (20%)
  between operations  13.9 us (7%)
  local copies, waits for them, and re-layouts  6.26 us (3%)
  matrix products  4.18 us (2%)
  other arithmetic  3.05 us (2%)
    psum x2, waiting for transfers between devices, from_root(): return lax.psum(block, axis)  85.2 us
    reduce_scatter x2, waiting for transfers between devices, refine(): share = lax.psum_scatter(product, 'col', scatter_dimension=0, tiled=True)  37.4 us
    all_gather x2, blocking collectives, refine(): return lax.all_gather(updated, 'col', axis=0, tiled=True)  26.7 us
    all_gather x1, blocking collectives, on_device(): col_joined = lax.all_gather(joined, 'row', axis=0, tiled=True)  10.8 us
    unnamed x22, local copies, waits for them, and re-layouts  4.4 us
  transfers between devices with their start and end apart: 4, of which 4 were waited for; matrix products, arithmetic and copies ran while one was open for 0% of the time, Pallas kernels for 0%

commit v1 on v0

--- a/solution.py
+++ b/solution.py
@@ -1,8 +1,11 @@
+import functools
 import math
 
 import jax
 import jax.numpy as jnp
 from jax import lax
+from jax.experimental import pallas as pl
+from jax.experimental.pallas import tpu as pltpu
 from jax.sharding import PartitionSpec as P
 
 SUBAP = 2048
@@ -16,7 +19,7 @@
     return lax.psum(block, axis)
 
 
-def on_device(telemetry, scales, bands, noise, start, target):
+def tiled_plan(telemetry, scales, bands, noise, start, target):
     frame_count = telemetry.shape[1]
     row_count = lax.axis_size("row")
     col_count = lax.axis_size("col")
@@ -95,18 +98,198 @@
     return (first, second)
 
 
+EDGE = 256
+
+
+def first_kernel(
+    sizes, ids, rates, mine, other, tile, low, first, weight, whole, noise_all
+):
+    rows_n, cols_n, chunk, height, panel, norm_count, hops = sizes
+    order = rows_n * cols_n * chunk
+    half = rows_n // 2
+    col_id, row_id = ids[0], ids[1]
+    core = row_id % 2
+    for pos in range(half):
+        for slot in range(cols_n):
+            home = ((hops[slot] ^ col_id) * rows_n + 2 * pos + core) * chunk
+            away = ((hops[slot] ^ col_id) * rows_n + 2 * pos + 1 - core) * chunk
+            part = pl.ds(slot * chunk, chunk)
+            whole[pl.ds(pl.multiple_of(home, chunk), chunk), :] = mine[pos, part, :]
+            whole[pl.ds(pl.multiple_of(away, chunk), chunk), :] = other[pos, part, :]
+    pieces = height // 128
+    scale = jnp.float32(1.0 / norm_count)
+    lanes = lax.broadcasted_iota(jnp.int32, (EDGE, 128), 1)
+    ramp_r = lax.broadcasted_iota(jnp.int32, (EDGE, EDGE), 0)
+    ramp_c = lax.broadcasted_iota(jnp.int32, (EDGE, EDGE), 1)
+    own = row_id // 2
+    parts = height // EDGE
+
+    def block(step, _):
+        pos = (own + 1 + step // parts) % half
+        piece = step % parts
+        base = (2 * pos + core) * height + piece * EDGE
+        sensor = base // SUBAP
+        place = base % SUBAP
+        rows = whole[pl.ds(pl.multiple_of(base, EDGE), EDGE), :]
+        only_s = jnp.where(lanes >= panel, rows, jnp.zeros_like(rows))
+        ramp = (ramp_r - ramp_c).astype(jnp.float32)
+        into = pl.ds(pl.multiple_of(piece * EDGE, EDGE), EDGE)
+        for col in range(order // EDGE):
+            cols = whole[pl.ds(col * EDGE, EDGE), :]
+            raw = lax.dot_general(
+                only_s, cols, (((1,), (1,)), ((), ())), preferred_element_type=jnp.float32
+            )
+            rate = rates[sensor, col * EDGE // SUBAP]
+            gap = (place - col * EDGE % SUBAP).astype(jnp.float32)
+            taper = jnp.maximum(0.0, scale - jnp.abs(ramp + gap) * (rate * scale))
+            tile[into, pl.ds(col * EDGE, EDGE)] = (taper * raw).astype(jnp.bfloat16)
+        cols = whole[pl.ds(pl.multiple_of(base, EDGE), EDGE), :]
+        raw = lax.dot_general(
+            only_s, cols, (((1,), (1,)), ((), ())), preferred_element_type=jnp.float32
+        )
+        planes = mine[pos, pl.ds(cols_n * chunk + height // 2, 16), :].astype(jnp.float32)
+        noises = planes[0:pieces] + planes[pieces : 2 * pieces] + planes[2 * pieces : 3 * pieces]
+        noise_all[0:pieces, :] = noises
+        line = jnp.concatenate(
+            [noise_all[pl.ds(piece * (EDGE // 128) + k, 1), :] for k in range(EDGE // 128)], axis=1
+        )
+        taper = jnp.maximum(0.0, scale - jnp.abs(ramp) * (rates[sensor, sensor] * scale))
+        diag = jnp.where(ramp_r == ramp_c, line, 0.0)
+        tile[into, pl.ds(pl.multiple_of(base, EDGE), EDGE)] = (taper * raw + diag).astype(jnp.bfloat16)
+        bottom = jnp.sum(jnp.where(ramp_r == ramp_c, raw * scale + line, 0.0), axis=1, keepdims=True)
+        wgt = damping / bottom
+        product = jnp.dot(tile[into, :], whole[...], preferred_element_type=jnp.float32)
+        pair = mine[pos, pl.ds(cols_n * chunk, height // 2), :]
+        side = jnp.where(piece * EDGE < height // 2, pair[:, 0:panel], pair[:, panel:])
+        goal = side.astype(jnp.float32)
+        new = rows[:, 0:panel].astype(jnp.float32) + wgt * (goal - product[:, 0:panel])
+        low[pos, into, :] = new.astype(jnp.bfloat16)
+        first[into, :] = new
+        weight[into, :] = jnp.broadcast_to(wgt, (EDGE, panel))
+        return 0
+
+    lax.fori_loop(0, half * parts, block, 0)
+
+
+def second_kernel(sizes, ids, tile, home, away, first, weight, target, second):
+    rows_n, cols_n, chunk, height, panel, norm_count, hops = sizes
+    core = ids[1] % 2
+    total = jnp.zeros((height, panel), jnp.float32)
+    for pos in range(rows_n // 2):
+        near = pl.multiple_of((2 * pos + core) * height, height)
+        far = pl.multiple_of((2 * pos + 1 - core) * height, height)
+        total += jnp.dot(tile[:, pl.ds(near, height)], home[pos], preferred_element_type=jnp.float32)
+        total += jnp.dot(tile[:, pl.ds(far, height)], away[pos], preferred_element_type=jnp.float32)
+    second[...] = first[...] + weight[...] * (target[...].astype(jnp.float32) - total)
+
+
+def flip(block, axis, bit):
+    size = lax.axis_size(axis)
+    return lax.ppermute(block, axis, [(i, i ^ bit) for i in range(size)])
+
+
+def gathered_plan(telemetry, scales, bands, noise, start, target):
+    rows_n = lax.axis_size("row")
+    cols_n = lax.axis_size("col")
+    chunk, frames = telemetry.shape
+    height, panel = target.shape
+    order = chunk * rows_n * cols_n
+    half = rows_n // 2
+    ids = jnp.stack([lax.axis_index("col"), lax.axis_index("row")]).astype(jnp.int32)
+    count = bands.shape[0]
+    index = jnp.arange(count, dtype=jnp.int32)
+    sym = jnp.where(index[:, None] <= index[None, :], bands, bands.T).astype(jnp.float32)
+    rates = 1.0 / sym
+    slopes = (telemetry.astype(jnp.float32) * scales.astype(jnp.float32)[:, None] / 128.0).astype(
+        jnp.bfloat16
+    )
+    block = jnp.concatenate([start, slopes], axis=1)
+    hops = (0,)
+    bit = cols_n // 2
+    while bit:
+        block = jnp.concatenate([block, flip(block, "col", bit)], axis=0)
+        hops = hops + tuple(hop ^ bit for hop in hops)
+        bit //= 2
+    sizes = (rows_n, cols_n, chunk, height, panel, float(order // 4), hops)
+    pair = jnp.concatenate([target[: height // 2], target[height // 2 :]], axis=1)
+    high = lax.reduce_precision(noise, 8, 7)
+    rest = noise - high
+    middle = lax.reduce_precision(rest, 8, 7)
+    planes = jnp.concatenate([high, middle, rest - middle]).astype(jnp.bfloat16).reshape(-1, 128)
+    planes = jnp.pad(planes, ((0, 16 - planes.shape[0]), (0, 0)))
+    payload = jnp.concatenate([block, pair, planes], axis=0)
+    groups = [list(range(k, rows_n, 2)) for k in range(2)]
+    mine = lax.all_gather(payload, "row", axis=0, axis_index_groups=groups)
+    other = flip(mine, "row", 1)
+    vmem = pl.BlockSpec(memory_space=pltpu.VMEM)
+    smem = pl.BlockSpec(memory_space=pltpu.SMEM)
+    tile, low, first, weight = pl.pallas_call(
+        functools.partial(first_kernel, sizes),
+        out_shape=(
+            jax.ShapeDtypeStruct((height, order), jnp.bfloat16),
+            jax.ShapeDtypeStruct((half, height, panel), jnp.bfloat16),
+            jax.ShapeDtypeStruct((height, panel), jnp.float32),
+            jax.ShapeDtypeStruct((height, panel), jnp.float32),
+        ),
+        in_specs=[smem, smem, vmem, vmem],
+        out_specs=(vmem, vmem, vmem, vmem),
+        scratch_shapes=[
+            pltpu.VMEM((order, 128), jnp.bfloat16),
+            pltpu.VMEM((8, 128), jnp.float32),
+        ],
+        compiler_params=pltpu.CompilerParams(vmem_limit_bytes=40 * 1024 * 1024),
+        name="first_pass",
+    )(ids, rates, mine, other)
+    away = flip(low, "row", 1)
+    second = pl.pallas_call(
+        functools.partial(second_kernel, sizes),
+        out_shape=jax.ShapeDtypeStruct((height, panel), jnp.float32),
+        in_specs=[smem, vmem, vmem, vmem, vmem, vmem, vmem],
+        out_specs=vmem,
+        compiler_params=pltpu.CompilerParams(vmem_limit_bytes=40 * 1024 * 1024),
+        name="second_pass",
+    )(ids, tile, low, away, first, weight, target)
+    return (first, second)
+
+
+def power_of_two(number):
+    return number > 0 and number & (number - 1) == 0
+
+
+def fits(mesh, telemetry, target):
+    rows_n, cols_n = mesh.shape["row"], mesh.shape["col"]
+    order, frames = telemetry.shape
+    panel = target.shape[1]
+    height = order // rows_n
+    return (
+        power_of_two(rows_n)
+        and power_of_two(cols_n)
+        and rows_n >= 2
+        and frames == panel == 64
+        and order % SUBAP == 0
+        and SUBAP % height == 0
+        and height == 2 * EDGE
+        and order // (rows_n * cols_n) % 16 == 0
+        and order <= 2 * SUBAP
+    )
+
+
 def solution(mesh):
-    return jax.shard_map(
-        on_device,
-        mesh=mesh,
-        in_specs=(
-            P(("col", "row"), None),
-            P(("col", "row")),
-            P(),
-            P("row"),
-            P(("col", "row"), None),
-            P("row", None),
-        ),
-        out_specs=(P("row", None), P("row", None)),
-        check_vma=False,
-    )
+    def program(telemetry, scales, bands, noise, start, target):
+        plan = gathered_plan if fits(mesh, telemetry, target) else tiled_plan
+        return jax.shard_map(
+            plan,
+            mesh=mesh,
+            in_specs=(
+                P(("col", "row"), None),
+                P(("col", "row")),
+                P(),
+                P("row"),
+                P(("col", "row"), None),
+                P("row", None),
+            ),
+            out_specs=(P("row", None), P("row", None)),
+            check_vma=False,
+        )(telemetry, scales, bands, noise, start, target)
+
+    return program

time: 188 us -> 53.9 us (0.29)
  waiting for transfers between devices: 123 us -> 4.15 us
  blocking collectives: 37.6 us -> 12.5 us
  Pallas kernels: 0 us -> 17.4 us
  between operations: 13.9 us -> 0.68 us
  starting transfers between devices: 0.16 us -> 5.78 us
  matrix products: 4.18 us -> 0 us
  local copies, waits for them, and re-layouts: 6.26 us -> 8.52 us
    psum x2 -> x0, waiting for transfers between devices: 85.2 us -> none  [from_root(): return lax.psum(block, axis)]
    reduce_scatter x2 -> x0, waiting for transfers between devices: 37.4 us -> none  [refine(): share = lax.psum_scatter(product, 'col', scatter_dimension=0, tiled=True)]
    all_gather x3 -> x1, blocking collectives: 37.6 us -> 12.5 us  [gathered_plan(): mine = lax.all_gather(payload, 'row', axis=0, axis_index_groups=groups)]
    pallas_call x0 -> x2, Pallas kernels: none -> 17.4 us  [the longest x1 15.6 us: gathered_plan(): pl.pallas_call(functools.partial(first_kernel, sizes), out_shape=(jax.Sha...]
    ppermute x0 -> x4, starting transfers between devices: none -> 5.78 us  [flip(): return lax.ppermute(block, axis, [(i, i ^ bit) for i in range(size)])]
    dot_general x5 -> x0, matrix products: 4.18 us -> none  [the longest x1 1.82 us: on_device(): product1 = jnp.dot(tile, col_first, preferred_element_type=jnp.float32)]
    ppermute x0 -> x4, waiting for transfers between devices: none -> 4.15 us  [flip(): return lax.ppermute(block, axis, [(i, i ^ bit) for i in range(size)])]
    unnamed x22 -> x10, local copies, waits for them, and re-layouts: 4.4 us -> 7.42 us
  transfers between devices with their start and end apart: 4 -> 4, of which waited for: 4 -> 3; matrix products, arithmetic and copies ran while one was open for 0% -> 9% of each run, Pallas kernels for 0% -> 0%
where the time goes in v1:
time: 53.9 us; the launch traced here: 53.4 us
  Pallas kernels  17.4 us (32%)
  blocking collectives  12.5 us (23%)
  local copies, waits for them, and re-layouts  8.52 us (16%)
  starting transfers between devices  5.78 us (11%)
  other arithmetic  4.34 us (8%)
  waiting for transfers between devices  4.15 us (8%)
  between operations  0.68 us (1%)
    pallas_call x1, Pallas kernels, gathered_plan(): pl.pallas_call(functools.partial(first_kernel, sizes), out_shape=(jax.Sha...  15.6 us
    all_gather x1, blocking collectives, gathered_plan(): mine = lax.all_gather(payload, 'row', axis=0, axis_index_groups=groups)  12.5 us
    unnamed x10, local copies, waits for them, and re-layouts  7.42 us
    ppermute x4, starting transfers between devices, flip(): return lax.ppermute(block, axis, [(i, i ^ bit) for i in range(size)])  5.78 us
    ppermute x4, waiting for transfers between devices, flip(): return lax.ppermute(block, axis, [(i, i ^ bit) for i in range(size)])  4.15 us
    pallas_call x1, Pallas kernels, gathered_plan(): pl.pallas_call(functools.partial(second_kernel, sizes), out_shape=jax.Sha...  1.79 us
  transfers between devices with their start and end apart: 4, of which 3 were waited for; matrix products, arithmetic and copies ran while one was open for 9% of the time, Pallas kernels for 0%

profile of v1, /device:TPU:0, one launch (start us, length us, event | category | flops | bytes accessed | tf_op | source)
XLA Modules:
  0.0 53.4 jit_solution(6879357822683144378)
XLA Ops:
  0.6 0.7 %convert_element_type.18 = f32[128]{0:T(128)S(1)} convert(s32[128]{0:T(128)} %param.7) | non-fusion elementwise | flops 128 | bytes 1024 | tf_op jit(solution)/shard_map/convert_element_type | solution.py:203
  1.3 0.8 %multiply_convert_fusion = bf16[128,64]{0,1:T(8,128)(2,1)S(1)} fusion(s32[128,64]{0,1:T(8,128)} %param.6, f32[128]{0:T(128)S(1)} %convert_element_type.18), kind=kLoop, calls=%fused_computation.4 | loop fusion | flops 32768 | bytes 49664 | tf_op jit(solution)/shard_map/convert_element_type | solution.py:203
  2.1 0.7 %pad_maximum_fusion.1 = (bf16[128,128]{0,1:T(8,128)(2,1)S(1)}, bf16[784,128]{0,1:T(8,128)(2,1)S(1)}) fusion(bf16[128,64]{0,1:T(8,128)(2,1)S(1)} %multiply_convert_fusion, bf16[128,64]{0,1:T(8,128)(2,1)} %param.10), kind=kLoop, calls=%fused_computation.2 | loop fusion | flops 65535 | bytes 98304 | tf_op jit(solution)/shard_map/concatenate | solution.py:206
  2.8 4.1 %collective-permute-start = (bf16[128,128]{0,1:T(8,128)(2,1)S(1)}, bf16[128,128]{0,1:T(8,128)(2,1)S(1)}, u32[]{:S(2)}, u32[]{:S(2)}) collective-permute-start(bf16[128,128]{0,1:T(8,128)(2,1)S(1)} %get-tuple-element.22), channel_id=1, source_target_pairs={{0,2},{1,3},{2,0},{3,1},{4,6},{5,7},{6,4},{7,5},{8,10},{9,11},{10,... | collective-permute-start | bytes 98312 | tf_op jit(solution)/shard_map/ppermute | solution.py:188
  6.9 0.8 %fusion.6 = (bf16[256,64]{0,1:T(8,128)(2,1)S(1)}, bf16[256,64]{0,1:T(8,128)(2,1)S(1)}) fusion(bf16[512,64]{0,1:T(8,128)(2,1)} %param.11), kind=kLoop, calls=%fused_computation.21 | loop fusion | bytes 131072 | tf_op jit(solution)/shard_map/slice | solution.py:214
  7.7 0.7 %fusion.4 = (bf16[4,128]{1,0:T(4,128)(2,1)S(1)}, bf16[4,128]{1,0:T(4,128)(2,1)S(1)}, bf16[4,128]{1,0:T(4,128)(2,1)S(1)}) fusion(f32[512]{0:T(512)} %param.9), kind=kLoop, calls=%fused_computation.18 | loop fusion | flops 3584 | bytes 5120 | tf_op jit(solution)/shard_map/concatenate | solution.py:218
  8.4 0.1 copy.36
  8.5 0.6 %collective-permute-done = bf16[128,128]{0,1:T(8,128)(2,1)S(1)} collective-permute-done((bf16[128,128]{0,1:T(8,128)(2,1)S(1)}, bf16[128,128]{0,1:T(8,128)(2,1)S(1)}, u32[]{:S(2)}, u32[]{:S(2)}) %collective-permute-start) | collective-permute-done | bytes 32800 | tf_op jit(solution)/shard_map/ppermute | solution.py:188
  9.1 0.7 %pad_maximum_fusion = bf16[256,128]{0,1:T(8,128)(2,1)S(1)} fusion(bf16[128,128]{0,1:T(8,128)(2,1)S(1)} %collective-permute-done, bf16[128,64]{0,1:T(8,128)(2,1)S(1)} %multiply_convert_fusion, bf16[128,64]{0,1:T(8,128)(2,1)} %param.10), kind=kLoop, calls=%fused_computation | loop fusion | flops 196608 | bytes 131072 | tf_op jit(solution)/shard_map/concatenate | solution.py:210
  9.8 1.6 %collective-permute-start.1 = (bf16[256,128]{0,1:T(8,128)(2,1)S(1)}, bf16[256,128]{0,1:T(8,128)(2,1)S(1)}, u32[]{:S(2)}, u32[]{:S(2)}) collective-permute-start(bf16[256,128]{0,1:T(8,128)(2,1)S(1)} %pad_maximum_fusion), channel_id=1, source_target_pairs={{0,1},{1,0},{2,3},{3,2},{4,5},{5,4},{6,7},{7,6},{8,9},{9,8},{10,11... | collective-permute-start | bytes 196616 | tf_op jit(solution)/shard_map/ppermute | solution.py:188
  11.4 2.7 %collective-permute-done.1 = bf16[256,128]{0,1:T(8,128)(2,1)S(1)} collective-permute-done((bf16[256,128]{0,1:T(8,128)(2,1)S(1)}, bf16[256,128]{0,1:T(8,128)(2,1)S(1)}, u32[]{:S(2)}, u32[]{:S(2)}) %collective-permute-start.1) | collective-permute-done | bytes 65568 | tf_op jit(solution)/shard_map/ppermute | solution.py:188
  14.2 0.2 copy.37
  14.3 12.5 %all-gather = bf16[3136,128]{1,0:T(8,128)(2,1)S(1)} all-gather(bf16[784,128]{1,0:T(8,128)(2,1)S(1)} %copy.37), channel_id=2, replica_groups={{0,8,16,24},{4,12,20,28},{1,9,17,25},{5,13,21,29},{2,10,18,26},{6,14,22..., dimensions={0}, use_global_device_ids=true | all-gather | bytes 1003520 | tf_op jit(solution)/shard_map/all_gather | solution.py:222
  26.9 0.0 collective-permute-start.2
  26.9 0.8 %copy.35 = s32[2,2]{0,1:T(2,128)S(1)} copy(s32[2,2]{1,0:T(2,128)} %param.8) | data formatting | bytes 32 | tf_op args[2]
  27.6 0.1 pad_add_fusion.ids
  27.7 0.7 %fusion.2.rates = f32[2,2]{1,0:T(2,128)S(1)} fusion(s32[2,2]{1,0:T(2,128)} %param.8, s32[2,2]{0,1:T(2,128)S(1)} %copy.35), kind=kLoop, calls=%fused_computation.16 | loop fusion | flops 16 | bytes 48 | tf_op jit(solution)/shard_map/div | solution.py:202
  28.4 0.8 %collective-permute-done.2.other = bf16[4,784,128]{2,1,0:T(8,128)(2,1)S(1)} collective-permute-done((bf16[4,784,128]{2,1,0:T(8,128)(2,1)S(1)}, bf16[4,784,128]{2,1,0:T(8,128)(2,1)S(1)}, u32[]{:S(2)}, u32[]{:S(2)}) %collective-permute-start.2) | collective-permute-done | bytes 802848 | tf_op jit(solution)/shard_map/ppermute | solution.py:188
  29.2 15.6 %first_pass.1 = (bf16[512,4096]{1,0:T(8,128)(2,1)S(1)}, bf16[4,512,64]{2,1,0:T(8,128)(2,1)S(1)}, f32[512,64]{1,0:T(8,128)S(1)}, f32[512,64]{1,0:T(8,128)S(1)}) custom-call(s32[2]{0:T(128)S(1)} %pad_add_fusion.ids, f32[2,2]{1,0:T(2,128)S(1)} %fusion.2.rates, bf16[4,784,128]{2,1,0:T(8,128)(2,1)S(1)} %bitcast.12, ...), custom_call_target="tpu_custom_call" | custom-call | tf_op jit(solution)/shard_map/first_pass/pallas_call | solution.py:226
  44.8 0.0 copy-start
  44.8 1.9 %copy-done = bf16[512,4096]{1,0:T(8,128)(2,1)} copy-done((bf16[512,4096]{1,0:T(8,128)(2,1)}, bf16[512,4096]{1,0:T(8,128)(2,1)S(1)}, u32[]{:S(2)}) %copy-start) | copy-done | bytes 4194328
  46.7 0.1 collective-permute-start.3
  46.9 1.0 %copy.38.target = bf16[512,64]{1,0:T(8,128)(2,1)S(1)} copy(bf16[512,64]{0,1:T(8,128)(2,1)} %param.11) | data formatting | bytes 131072 | tf_op args[5]
  47.8 0.8 %copy.39 = f32[512,64]{0,1:T(8,128)} copy(f32[512,64]{1,0:T(8,128)S(1)} %get-tuple-element.18.first) | data formatting | bytes 262144
  48.6 0.0 collective-permute-done.3.away
  48.6 0.0 copy-start.1
  48.6 2.2 %copy-done.1 = bf16[512,4096]{1,0:T(8,128)(2,1)S(1)} copy-done((bf16[512,4096]{1,0:T(8,128)(2,1)S(1)}, bf16[512,4096]{1,0:T(8,128)(2,1)}, u32[]{:S(2)}) %copy-start.1) | copy-done | bytes 4194328
  50.8 1.8 %second_pass.1 = f32[512,64]{1,0:T(8,128)S(1)} custom-call(s32[2]{0:T(128)S(1)} %pad_add_fusion.ids, bf16[512,4096]{1,0:T(8,128)(2,1)S(1)} %copy-done.1, bf16[4,512,64]{2,1,0:T(8,128)(2,1)S(1)} %get-tuple-element.8.home, bf16[4,512,64]{2,1,0:T(8,128)(2,1)S(1)} %collective-permute-done.3.away, f32[512,64]{1,0:T(8,128)S(1)} %get-tuple-element.18.first, ...), custom_call_target="tpu_custom_call" | custom-call | tf_op jit(solution)/shard_map/second_pass/pallas_call | solution.py:244
  52.6 0.8 %copy.40 = f32[512,64]{0,1:T(8,128)} copy(f32[512,64]{1,0:T(8,128)S(1)} %second_pass.1) | data formatting | bytes 262144
  (5 shorter events, 0.1 us)
Async XLA Ops:
  2.8 6.3 %collective-permute-start = (bf16[128,128]{0,1:T(8,128)(2,1)S(1)}, bf16[128,128]{0,1:T(8,128)(2,1)S(1)}, u32[]{:S(2)}, u32[]{:S(2)}) collective-permute-start(bf16[128,128]{0,1:T(8,128)(2,1)S(1)} %get-tuple-element.22), channel_id=1, source_target_pairs={{0,2},{1,3},{2,0},{3,1},{4,6},{5,7},{6,4},{7,5},{8,10},{9,11},{10,... | collective-permute-start | bytes 98312 | tf_op jit(solution)/shard_map/ppermute | solution.py:188
  9.8 4.3 %collective-permute-start.1 = (bf16[256,128]{0,1:T(8,128)(2,1)S(1)}, bf16[256,128]{0,1:T(8,128)(2,1)S(1)}, u32[]{:S(2)}, u32[]{:S(2)}) collective-permute-start(bf16[256,128]{0,1:T(8,128)(2,1)S(1)} %pad_maximum_fusion), channel_id=1, source_target_pairs={{0,1},{1,0},{2,3},{3,2},{4,5},{5,4},{6,7},{7,6},{8,9},{9,8},{10,11... | collective-permute-start | bytes 196616 | tf_op jit(solution)/shard_map/ppermute | solution.py:188
  26.9 2.3 %collective-permute-start.2 = (bf16[4,784,128]{2,1,0:T(8,128)(2,1)S(1)}, bf16[4,784,128]{2,1,0:T(8,128)(2,1)S(1)}, u32[]{:S(2)}, u32[]{:S(2)}) collective-permute-start(bf16[4,784,128]{2,1,0:T(8,128)(2,1)S(1)} %bitcast.11), channel_id=1, source_target_pairs={{0,4},{4,0},{8,12},{12,8},{16,20},{20,16},{24,28},{28,24},{1,5},{5... | collective-permute-start | bytes 2408456 | tf_op jit(solution)/shard_map/ppermute | solution.py:188
  44.8 1.9 %copy-start = (bf16[512,4096]{1,0:T(8,128)(2,1)}, bf16[512,4096]{1,0:T(8,128)(2,1)S(1)}, u32[]{:S(2)}) copy-start(bf16[512,4096]{1,0:T(8,128)(2,1)S(1)} %get-tuple-element.7.tile) | copy-start | bytes 12582916
  46.7 1.9 %collective-permute-start.3 = (bf16[4,512,64]{2,1,0:T(8,128)(2,1)S(1)}, bf16[4,512,64]{2,1,0:T(8,128)(2,1)S(1)}, u32[]{:S(2)}, u32[]{:S(2)}) collective-permute-start(bf16[4,512,64]{2,1,0:T(8,128)(2,1)S(1)} %get-tuple-element.8.home), channel_id=1, source_target_pairs={{0,4},{4,0},{8,12},{12,8},{16,20},{20,16},{24,28},{28,24},{1,5},{5... | collective-permute-start | bytes 786440 | tf_op jit(solution)/shard_map/ppermute | solution.py:188
  48.6 2.2 %copy-start.1 = (bf16[512,4096]{1,0:T(8,128)(2,1)S(1)}, bf16[512,4096]{1,0:T(8,128)(2,1)}, u32[]{:S(2)}) copy-start(bf16[512,4096]{1,0:T(8,128)(2,1)} %copy-done) | copy-start | bytes 12582916
